TPU v7x, 256 devices: a whole 4x4x8 slice. The times are simulated.
256 devices in a mesh: row: 8 (over z_hi, core), col: 32 (over z_lo, y, x).
Axes of the slice: x: 4, y: 4, z: 8 (z_hi: 4, z_lo: 2; z = z_hi * 2 + z_lo), core: 2. Of those that a mesh axis runs over, the one named last changes fastest.
Arguments:
- tiles: bfloat16 [8, 32, 256, 128, 128], P('row', 'col'), may hold values from -0.046875 to 0.046875
- block_rows: int32 [8, 32, 256], P('row', 'col'), may hold values from 0 to 7
- block_cols: int32 [8, 32, 256], P('row', 'col'), may hold values from 0 to 31
- live: int32 [8, 32], P('row', 'col'), may hold values from 32 to 256, as said below
- seeds: float32 [32768, 64], P(('col', 'row')), may hold values from -6 to 6
- beta: float32 [64], replicated, may hold values from 0.3 to 0.9
Outputs:
- scores: float32 [32768, 64], P(('col', 'row'))
Inputs may be any that keep to these rules, and one draw needn't show every extreme that they name: Some device has all 256 slots live and some device exactly 32; live counts differ strongly between devices.
All inputs are finite; a program needn't handle non-finite values.
Results may differ from a plain program's by a relative error of at most 0.0039.
Values may be sent and summed in bfloat16 or wider, within the bound.
A program may use at most 64 MiB of HBM per device.

v0:
```python
import jax
import jax.numpy as jnp
from jax import lax
from jax.sharding import PartitionSpec as P

TERMS = 4


GROUP_SLOTS = 16


def add_group(tiles, brow, bcol, usable, across, downward, start, totals):
    blk = tiles.shape[1]
    width = across.shape[1]
    row_blocks = totals[0].shape[0]
    col_blocks = totals[1].shape[0]
    tile = lax.dynamic_slice_in_dim(tiles, start, GROUP_SLOTS, 0)
    rows = lax.dynamic_slice_in_dim(brow, start, GROUP_SLOTS, 0)
    cols = lax.dynamic_slice_in_dim(bcol, start, GROUP_SLOTS, 0)
    keep = lax.dynamic_slice_in_dim(usable, start, GROUP_SLOTS, 0).astype(jnp.float32)[
        :, None, None
    ]
    incoming = across.reshape(col_blocks, blk, width)[cols]
    fwd = jnp.einsum("sij,sjk->sik", tile, incoming, preferred_element_type=jnp.float32) * keep
    lowered = downward.reshape(row_blocks, blk, width)[rows]
    bwd = jnp.einsum("sji,sjk->sik", tile, lowered, preferred_element_type=jnp.float32) * keep
    forward = totals[0] + jax.ops.segment_sum(fwd, rows, row_blocks)
    backward = totals[1] + jax.ops.segment_sum(bwd, cols, col_blocks)
    return (forward, backward)


def shards(tiles, block_rows, block_cols, live, seeds, beta):
    tiles = tiles[0, 0]
    brow = block_rows[0, 0]
    bcol = block_cols[0, 0]
    filled = live[0, 0]
    slots = tiles.shape[0]
    blk = tiles.shape[1]
    piece = seeds.shape[0]
    width = seeds.shape[1]
    row_blocks = lax.axis_size("row") * piece // blk
    col_blocks = lax.axis_size("col") * piece // blk
    usable = jnp.arange(slots, dtype=jnp.int32) < filled
    scores = seeds
    for term in range(TERMS):
        current = scores.astype(jnp.bfloat16)
        across = lax.all_gather(current, "col", axis=0, tiled=True)
        downward = lax.all_gather(current, "row", axis=0, tiled=True)

        def one_group(group, totals):
            return add_group(
                tiles, brow, bcol, usable, across, downward, group * GROUP_SLOTS, totals
            )

        start_sums = (
            jnp.zeros((row_blocks, blk, width), jnp.float32),
            jnp.zeros((col_blocks, blk, width), jnp.float32),
        )
        forward, backward = lax.fori_loop(0, slots // GROUP_SLOTS, one_group, start_sums)
        forward = forward.reshape(row_blocks * blk, width)
        backward = backward.reshape(col_blocks * blk, width)
        forward_piece = lax.psum_scatter(forward, "row", scatter_dimension=0, tiled=True)
        backward_piece = lax.psum_scatter(backward, "col", scatter_dimension=0, tiled=True)
        scores = beta[None, :] * (forward_piece + backward_piece) + seeds
    return scores


def solution(mesh):
    placed = (
        P("row", "col", None, None, None),
        P("row", "col", None),
        P("row", "col", None),
        P("row", "col"),
        P(("col", "row"), None),
        P(),
    )
    return jax.shard_map(
        shards, mesh=mesh, in_specs=placed, out_specs=P(("col", "row"), None), check_vma=False
    )
```

profile of v0, /device:TPU:1, one launch (start us, length us, event | category | flops | bytes accessed | tf_op | source)
XLA Modules:
  0.0 1664.4 jit_solution(6240223318505519439)
XLA Ops:
  7.3 71.7 %all_gather.24 = bf16[4096,64]{0,1:T(8,128)(2,1)S(1)} all-gather(bf16[128,64]{0,1:T(8,128)(2,1)S(1)} %convert_element_type.40), channel_id=1, replica_groups=mesh['row'=8,'col'=32] {'col'}, dimensions={0}, use_global_device_ids=true | all-gather | bytes 540672 | tf_op jit(solution)/shard_map/all_gather | solution.py:47
  79.0 31.5 %all_gather.25 = bf16[1024,64]{0,1:T(8,128)(2,1)S(1)} all-gather(bf16[128,64]{0,1:T(8,128)(2,1)S(1)} %convert_element_type.40), channel_id=1, replica_groups=mesh['row'=8,'col'=32] {'row'}, dimensions={0}, use_global_device_ids=true | all-gather | bytes 147456 | tf_op jit(solution)/shard_map/all_gather | solution.py:48
  111.4 124.9 %while.60 = (s32[]{:T(128)}, f32[8,128,64]{1,2,0:T(8,128)S(1)}, f32[32,128,64]{1,2,0:T(8,128)S(1)}, s32[256]{0:T(256)}, bf16[256,128,128]{2,1,0:T(8,128)(2,1)}, ...) while((s32[]{:T(128)}, f32[8,128,64]{1,2,0:T(8,128)S(1)}, ...), condition=%wide.region_3.0_spmd, body=%wide.region_0.0_spmd.sunk | while | flops 67635312 | bytes 8135819 | solution.py:59
  116.3 1.5 convolution_multiply_fusion.16
  124.1 1.5 convolution_multiply_fusion.16
  155.4 1.5 convolution_multiply_fusion.16
  202.2 1.5 convolution_multiply_fusion.16
  210.0 1.5 convolution_multiply_fusion.16
  233.4 1.5 convolution_multiply_fusion.16
  238.2 26.9 %reduce-scatter.9.cloned.1.call-done = f32[128,64]{0,1:T(8,128)} async-done(((f32[1024,64]{0,1:T(8,128)}), f32[128,64]{0,1:T(8,128)}) %reduce-scatter.9.cloned.1.call-update) | async-done | bytes 32784 | tf_op jit(solution)/shard_map/reduce_scatter | solution.py:62
  265.1 140.2 %reduce-scatter.11.cloned.1.call-done = f32[128,64]{0,1:T(8,128)} async-done(((f32[4096,64]{0,1:T(8,128)}), f32[128,64]{0,1:T(8,128)}) %reduce-scatter.11.cloned.1.call-update) | async-done | bytes 32784 | tf_op jit(solution)/shard_map/reduce_scatter | solution.py:63
  406.2 66.3 %all_gather.26 = bf16[4096,64]{0,1:T(8,128)(2,1)S(1)} all-gather(bf16[128,64]{0,1:T(8,128)(2,1)S(1)} %add_convert_fusion.2), channel_id=1, replica_groups=mesh['row'=8,'col'=32] {'col'}, dimensions={0}, use_global_device_ids=true | all-gather | bytes 540672 | tf_op jit(solution)/shard_map/all_gather | solution.py:47
  472.5 55.3 %all_gather.27 = bf16[1024,64]{0,1:T(8,128)(2,1)S(1)} all-gather(bf16[128,64]{0,1:T(8,128)(2,1)S(1)} %add_convert_fusion.2), channel_id=1, replica_groups=mesh['row'=8,'col'=32] {'row'}, dimensions={0}, use_global_device_ids=true | all-gather | bytes 147456 | tf_op jit(solution)/shard_map/all_gather | solution.py:48
  527.9 124.9 %while.61 = (s32[]{:T(128)}, f32[8,128,64]{1,2,0:T(8,128)S(1)}, f32[32,128,64]{1,2,0:T(8,128)S(1)}, s32[256]{0:T(256)}, bf16[256,128,128]{2,1,0:T(8,128)(2,1)}, ...) while((s32[]{:T(128)}, f32[8,128,64]{1,2,0:T(8,128)S(1)}, ...), condition=%wide.region_9.0_spmd, body=%wide.region_6.0_spmd.sunk | while | flops 67635312 | bytes 8135819 | solution.py:59
  540.7 1.5 convolution_multiply_fusion.18
  587.5 1.5 convolution_multiply_fusion.18
  603.2 1.5 convolution_multiply_fusion.18
  618.8 1.5 convolution_multiply_fusion.18
  634.4 1.5 convolution_multiply_fusion.18
  642.2 1.5 convolution_multiply_fusion.18
  654.8 26.9 %reduce-scatter.13.cloned.1.call-done = f32[128,64]{0,1:T(8,128)} async-done(((f32[1024,64]{0,1:T(8,128)}), f32[128,64]{0,1:T(8,128)}) %reduce-scatter.13.cloned.1.call-update) | async-done | bytes 32784 | tf_op jit(solution)/shard_map/reduce_scatter | solution.py:62
  681.8 140.9 %reduce-scatter.15.cloned.1.call-done = f32[128,64]{0,1:T(8,128)} async-done(((f32[4096,64]{0,1:T(8,128)}), f32[128,64]{0,1:T(8,128)}) %reduce-scatter.15.cloned.1.call-update) | async-done | bytes 32784 | tf_op jit(solution)/shard_map/reduce_scatter | solution.py:63
  823.5 64.5 %all_gather.28 = bf16[4096,64]{0,1:T(8,128)(2,1)S(1)} all-gather(bf16[128,64]{0,1:T(8,128)(2,1)S(1)} %add_convert_fusion.1), channel_id=1, replica_groups=mesh['row'=8,'col'=32] {'col'}, dimensions={0}, use_global_device_ids=true | all-gather | bytes 540672 | tf_op jit(solution)/shard_map/all_gather | solution.py:47
  888.0 56.1 %all_gather.29 = bf16[1024,64]{0,1:T(8,128)(2,1)S(1)} all-gather(bf16[128,64]{0,1:T(8,128)(2,1)S(1)} %add_convert_fusion.1), channel_id=1, replica_groups=mesh['row'=8,'col'=32] {'row'}, dimensions={0}, use_global_device_ids=true | all-gather | bytes 147456 | tf_op jit(solution)/shard_map/all_gather | solution.py:48
  944.2 124.9 %while.62 = (s32[]{:T(128)}, f32[8,128,64]{1,2,0:T(8,128)S(1)}, f32[32,128,64]{1,2,0:T(8,128)S(1)}, s32[256]{0:T(256)}, bf16[256,128,128]{2,1,0:T(8,128)(2,1)}, ...) while((s32[]{:T(128)}, f32[8,128,64]{1,2,0:T(8,128)S(1)}, ...), condition=%wide.region_15.0_spmd, body=%wide.region_12.0_spmd.sunk | while | flops 67635312 | bytes 8135819 | solution.py:59
  949.2 1.5 convolution_multiply_fusion.20
  957.0 1.5 convolution_multiply_fusion.20
  972.6 1.5 convolution_multiply_fusion.20
  988.2 1.5 convolution_multiply_fusion.20
  996.0 1.5 convolution_multiply_fusion.20
  1035.0 1.5 convolution_multiply_fusion.20
  1042.8 1.5 convolution_multiply_fusion.20
  1066.3 1.5 convolution_multiply_fusion.20
  1071.1 27.4 %reduce-scatter.17.cloned.1.call-done = f32[128,64]{0,1:T(8,128)} async-done(((f32[1024,64]{0,1:T(8,128)}), f32[128,64]{0,1:T(8,128)}) %reduce-scatter.17.cloned.1.call-update) | async-done | bytes 32784 | tf_op jit(solution)/shard_map/reduce_scatter | solution.py:62
  1098.4 140.4 %reduce-scatter.19.cloned.1.call-done = f32[128,64]{0,1:T(8,128)} async-done(((f32[4096,64]{0,1:T(8,128)}), f32[128,64]{0,1:T(8,128)}) %reduce-scatter.19.cloned.1.call-update) | async-done | bytes 32784 | tf_op jit(solution)/shard_map/reduce_scatter | solution.py:63
  1239.7 66.1 %all_gather.30 = bf16[4096,64]{0,1:T(8,128)(2,1)S(1)} all-gather(bf16[128,64]{0,1:T(8,128)(2,1)S(1)} %add_convert_fusion), channel_id=1, replica_groups=mesh['row'=8,'col'=32] {'col'}, dimensions={0}, use_global_device_ids=true | all-gather | bytes 540672 | tf_op jit(solution)/shard_map/all_gather | solution.py:47
  1305.8 55.3 %all_gather.31 = bf16[1024,64]{0,1:T(8,128)(2,1)S(1)} all-gather(bf16[128,64]{0,1:T(8,128)(2,1)S(1)} %add_convert_fusion), channel_id=1, replica_groups=mesh['row'=8,'col'=32] {'row'}, dimensions={0}, use_global_device_ids=true | all-gather | bytes 147456 | tf_op jit(solution)/shard_map/all_gather | solution.py:48
  1361.2 124.9 %while.63 = (s32[]{:T(128)}, f32[8,128,64]{1,2,0:T(8,128)S(1)}, f32[32,128,64]{1,2,0:T(8,128)S(1)}, s32[256]{0:T(256)}, bf16[256,128,128]{2,1,0:T(8,128)(2,1)}, ...) while((s32[]{:T(128)}, f32[8,128,64]{1,2,0:T(8,128)S(1)}, ...), condition=%wide.region_21.0_spmd, body=%wide.region_18.0_spmd.sunk | while | flops 67635312 | bytes 8135819 | solution.py:59
  1366.1 1.5 convolution_multiply_fusion.22
  1373.9 1.5 convolution_multiply_fusion.22
  1389.6 1.5 convolution_multiply_fusion.22
  1405.2 1.5 convolution_multiply_fusion.22
  1413.0 1.5 convolution_multiply_fusion.22
  1452.0 1.5 convolution_multiply_fusion.22
  1459.8 1.5 convolution_multiply_fusion.22
  1483.2 1.5 convolution_multiply_fusion.22
  1488.0 26.9 %reduce-scatter.21.cloned.1.call-done = f32[128,64]{0,1:T(8,128)} async-done(((f32[1024,64]{0,1:T(8,128)}), f32[128,64]{0,1:T(8,128)}) %reduce-scatter.21.cloned.1.call-update) | async-done | bytes 32784 | tf_op jit(solution)/shard_map/reduce_scatter | solution.py:62
  1514.8 141.3 %reduce-scatter.23.cloned.1.call-done = f32[128,64]{0,1:T(8,128)} async-done(((f32[4096,64]{0,1:T(8,128)}), f32[128,64]{0,1:T(8,128)}) %reduce-scatter.23.cloned.1.call-update) | async-done | bytes 32784 | tf_op jit(solution)/shard_map/reduce_scatter | solution.py:63
  (782 shorter events, 465.0 us)
Async XLA Ops:
  6.5 258.6 %reduce-scatter.9.cloned.1.call-start = ((), (), s32[]{:S(2)}) async-start(), calls=%async_computation.8 | async-start | bytes 294912 | tf_op jit(solution)/shard_map/reduce_scatter | solution.py:62
  111.4 294.0 %copy-start = (f32[128,64]{0,1:T(8,128)S(1)}, f32[128,64]{0,1:T(8,128)}, u32[]{:S(2)}) copy-start(f32[128,64]{0,1:T(8,128)} %param.18) | copy-start | bytes 98308
  111.4 294.0 %copy-start.1 = (f32[64]{0:T(128)S(1)}, f32[64]{0:T(128)}, u32[]{:S(2)}) copy-start(f32[64]{0:T(128)} %param.19) | copy-start | bytes 772
  237.0 168.3 %reduce-scatter.11.cloned.1.call-start = ((), (), s32[]{:S(2)}) async-start(), calls=%async_computation.9 | async-start | bytes 1081344 | tf_op jit(solution)/shard_map/reduce_scatter | solution.py:63
  238.2 443.6 %reduce-scatter.13.cloned.1.call-start = ((), (), s32[]{:S(2)}) async-start(), calls=%async_computation.10 | async-start | bytes 294912 | tf_op jit(solution)/shard_map/reduce_scatter | solution.py:62
  653.6 169.0 %reduce-scatter.15.cloned.1.call-start = ((), (), s32[]{:S(2)}) async-start(), calls=%async_computation.11 | async-start | bytes 1081344 | tf_op jit(solution)/shard_map/reduce_scatter | solution.py:63
  654.8 443.7 %reduce-scatter.17.cloned.1.call-start = ((), (), s32[]{:S(2)}) async-start(), calls=%async_computation.12 | async-start | bytes 294912 | tf_op jit(solution)/shard_map/reduce_scatter | solution.py:62
  1069.9 168.9 %reduce-scatter.19.cloned.1.call-start = ((), (), s32[]{:S(2)}) async-start(), calls=%async_computation.13 | async-start | bytes 1081344 | tf_op jit(solution)/shard_map/reduce_scatter | solution.py:63
  1071.0 443.8 %reduce-scatter.21.cloned.1.call-start = ((), (), s32[]{:S(2)}) async-start(), calls=%async_computation.14 | async-start | bytes 294912 | tf_op jit(solution)/shard_map/reduce_scatter | solution.py:62
  1486.9 169.3 %reduce-scatter.23.cloned.1.call-start = ((), (), s32[]{:S(2)}) async-start(), calls=%async_computation.15 | async-start | bytes 1081344 | tf_op jit(solution)/shard_map/reduce_scatter | solution.py:63
Sparse Core Ops, SparseCore 0:
  237.2 27.9 reduce-scatter.8
  267.8 137.5 reduce-scatter.10
  653.8 27.9 reduce-scatter.12
  684.3 138.3 reduce-scatter.14
  1070.0 28.3 reduce-scatter.16
  1101.0 137.8 reduce-scatter.18
  1487.0 27.8 reduce-scatter.20
  1517.5 138.5 reduce-scatter.22
where the time goes:
time: 1690 us; the launch traced here: 1660 us
  waiting for transfers between devices  671 us (40%)
  blocking collectives  467 us (28%)
  other arithmetic  232 us (14%)
  matrix products  180 us (11%)
  local copies, waits for them, and re-layouts  94.4 us (6%)
    reduce_scatter x4, waiting for transfers between devices, shards(): lax.psum_scatter(backward, 'col', scatter_dimension=0, tiled=True)  563 us
    all_gather x4, blocking collectives, shards(): across = lax.all_gather(current, 'col', axis=0, tiled=True)  269 us
    all_gather x4, blocking collectives, shards(): downward = lax.all_gather(current, 'row', axis=0, tiled=True)  198 us
    reduce_scatter x4, waiting for transfers between devices, shards(): lax.psum_scatter(forward, 'row', scatter_dimension=0, tiled=True)  108 us
    dot_general x64, matrix products, add_group(): jnp.einsum('sij,sjk->sik', tile, incoming, preferred_element_type=jnp.flo...  96.3 us
    scatter-add x64, other arithmetic, add_group(): forward = totals[0] + jax.ops.segment_sum(fwd, rows, row_blocks)  86.1 us
    scatter-add x64, other arithmetic, add_group(): backward = totals[1] + jax.ops.segment_sum(bwd, cols, col_blocks)  85.8 us
    dot_general x64, matrix products, add_group(): jnp.einsum('sji,sjk->sik', tile, lowered, preferred_element_type=jnp.floa...  83.7 us
  transfers between devices with their start and end apart: 8, of which 8 were waited for; matrix products, arithmetic and copies ran while one was open for 0% of the time, Pallas kernels for 0%

commit v1 on v0

v1 whole, which is shorter than its diff:
```python
import functools

import jax
import jax.numpy as jnp
from jax import lax
from jax.experimental import pallas as pl
from jax.experimental.pallas import tpu as pltpu
from jax.sharding import PartitionSpec as P

TERMS = 4
MESH = pl.DeviceIdType.MESH
F32 = jnp.float32
BF16 = jnp.bfloat16
LAST = (((1,), (1,)), ((), ()))

XZ, XROW, XOWN, XOTHER, POTHER, POWN, PROW, PZ = range(8)


def kernel(
    side,
    idx,
    tiles,
    seeds,
    beta,
    out,
    raw,
    run,
    dense,
    xs,
    ys,
    bstage,
    fstage,
    bland,
    fland,
    zstage,
    zland,
    facc,
    seeds_t,
    beta_t,
    score,
    tile_sem,
    send_sem,
    recv_sem,
):
    slots = raw.shape[0]
    blk = raw.shape[1]
    n_row = ys.shape[1]
    n_col = xs.shape[1]
    plane = side * side
    parts = tile_sem.shape[0]
    chunk = slots // parts
    r = lax.axis_index("row")
    c = lax.axis_index("col")
    z = c // plane
    yx = c % plane
    y = yx // side
    x = yx % side
    partner = ((z + 1) % 2) * plane + yx

    def plane_peer(off):
        return ((y + off // side) % side) * side + (x + off % side) % side

    def row_peer(off):
        return (r + off) % n_row

    def tile_copy(i):
        part = pl.ds(i * chunk, chunk)
        return pltpu.make_async_copy(tiles.at[part], raw.at[part], tile_sem.at[i])

    for i in range(parts):
        tile_copy(i).start()

    def send(src, dst, t, kind, device):
        pltpu.make_async_remote_copy(
            src_ref=src,
            dst_ref=dst,
            send_sem=send_sem.at[t, kind],
            recv_sem=recv_sem.at[t, kind],
            device_id=device,
            device_id_type=MESH,
        ).start()

    def await_bytes(ref, sem):
        pltpu.make_async_copy(ref, ref, sem).wait()

    barrier = pltpu.get_barrier_semaphore()
    pl.semaphore_signal(barrier, inc=1, device_id=(r, partner), device_id_type=MESH)

    @pl.loop(1, plane)
    def _(off):
        pl.semaphore_signal(
            barrier, inc=1, device_id=(r, z * plane + plane_peer(off)), device_id_type=MESH
        )

    @pl.loop(1, n_row)
    def _(off):
        pl.semaphore_signal(barrier, inc=1, device_id=(row_peer(off), c), device_id_type=MESH)

    seeds_t[...] = seeds[...].T
    beta_t[...] = jnp.broadcast_to(beta[...], (blk, beta.shape[1])).T
    score[...] = seeds_t[...]
    pl.semaphore_wait(barrier, 1 + (plane - 1) + (n_row - 1))

    def spread(t):
        current = score[...].astype(BF16)
        xs[t, c] = current
        ys[t, r] = current
        send(xs.at[t, c], xs.at[t, c], t, XZ, (r, partner))

        @pl.loop(1, n_row)
        def _(off):
            send(ys.at[t, r], ys.at[t, r], t, XROW, (row_peer(off), c))

        @pl.loop(1, plane)
        def _(off):
            send(xs.at[t, c], xs.at[t, c], t, XOWN, (r, z * plane + plane_peer(off)))

        await_bytes(xs.at[t, pl.ds(0, 1)], recv_sem.at[t, XZ])

        @pl.loop(1, plane)
        def _(off):
            send(xs.at[t, partner], xs.at[t, partner], t, XOTHER, (r, z * plane + plane_peer(off)))

    def densify():
        for i in range(parts):
            tile_copy(i).wait()

        def add(i, total):
            total = raw[idx[0, i]].astype(F32) + total * idx[1, i].astype(F32)
            run[i] = total.astype(BF16)
            return total

        lax.fori_loop(0, slots, add, jnp.zeros((blk, blk), F32), unroll=4)

        @pl.loop(0, n_col)
        def _(cb):
            for rb in range(n_row):
                p = rb * n_col + cb
                dense[cb, rb * blk : (rb + 1) * blk, :] = run[idx[2, p]] * idx[3, p].astype(BF16)

    def transposed(t, half, slot, kind):
        down = jnp.concatenate([ys[t, i] for i in range(n_row)], axis=1)

        def pair(g):
            first = half * plane + plane_peer(2 * g)
            second = half * plane + plane_peer(2 * g + 1)
            a = jnp.concatenate([dense[first], dense[second]], axis=1)
            return jnp.dot(down, a, preferred_element_type=F32).astype(BF16)

        def ship(off):
            send(
                bstage.at[slot, off],
                bland.at[t, slot, off - 1],
                t,
                kind,
                (r, z * plane + plane_peer(off)),
            )

        part = pair(0)
        bland[t, slot, plane - 1] = part[:, :blk]
        bstage[slot, 1] = part[:, blk:]
        ship(1)

        @pl.loop(1, plane // 2)
        def _(g):
            part = pair(g)
            bstage[slot, 2 * g] = part[:, :blk]
            bstage[slot, 2 * g + 1] = part[:, blk:]
            ship(2 * g)
            ship(2 * g + 1)

    def forward(t, half, last):
        @pl.loop(0, n_row // 2)
        def _(m):
            rows = pl.ds(pl.multiple_of(m * 2 * blk, 2 * blk), 2 * blk)
            total = facc[m] if last else jnp.zeros(facc.shape[1:], F32)
            for p in range(plane // 2):
                at = half * plane + 2 * p
                a = jnp.concatenate([dense[at, rows, :], dense[at + 1, rows, :]], axis=1)
                v = jnp.concatenate([xs[t, at], xs[t, at + 1]], axis=1)
                total = total + lax.dot_general(a, v, LAST, preferred_element_type=F32)
            if last:
                total = total.T.astype(BF16)
                fstage[2 * m] = total[:, :blk]
                fstage[2 * m + 1] = total[:, blk:]
            else:
                facc[m] = total

    def total_of(land, t, count):
        total = land[t, 0].astype(F32)
        for i in range(1, count):
            total = total + land[t, i].astype(F32)
        return total

    def term(t):
        other = (z + 1) % 2
        await_bytes(ys.at[t, pl.ds(0, n_row - 1)], recv_sem.at[t, XROW])
        transposed(t, other, 0, POTHER)
        transposed(t, z, 1, POWN)
        await_bytes(xs.at[t, pl.ds(0, plane - 1)], recv_sem.at[t, XOWN])
        forward(t, z, False)
        await_bytes(xs.at[t, pl.ds(0, plane - 1)], recv_sem.at[t, XOTHER])
        forward(t, other, True)
        fland[t, n_row - 1] = fstage[r]

        @pl.loop(1, n_row)
        def _(off):
            to = row_peer(off)
            send(fstage.at[to], fland.at[t, off - 1], t, PROW, (to, c))

        await_bytes(bland.at[t, 0, pl.ds(0, plane - 1)], recv_sem.at[t, POTHER])
        zstage[...] = total_of(bland.at[:, 0], t, plane)
        send(zstage, zland.at[t], t, PZ, (r, partner))
        await_bytes(bland.at[t, 1, pl.ds(0, plane - 1)], recv_sem.at[t, POWN])
        total = total_of(bland.at[:, 1], t, plane)
        await_bytes(fland.at[t, pl.ds(0, n_row - 1)], recv_sem.at[t, PROW])
        total = total + total_of(fland, t, n_row)
        await_bytes(zland.at[t], recv_sem.at[t, PZ])
        total = total + zland[t]
        score[...] = beta_t[...] * total + seeds_t[...]

        await_bytes(xs.at[t, pl.ds(0, 1)], send_sem.at[t, XZ])
        await_bytes(ys.at[t, pl.ds(0, n_row - 1)], send_sem.at[t, XROW])
        await_bytes(xs.at[t, pl.ds(0, plane - 1)], send_sem.at[t, XOWN])
        await_bytes(xs.at[t, pl.ds(0, plane - 1)], send_sem.at[t, XOTHER])
        await_bytes(bland.at[t, 0, pl.ds(0, plane - 1)], send_sem.at[t, POTHER])
        await_bytes(bland.at[t, 1, pl.ds(0, plane - 1)], send_sem.at[t, POWN])
        await_bytes(fland.at[t, pl.ds(0, n_row - 1)], send_sem.at[t, PROW])
        await_bytes(zland.at[t], send_sem.at[t, PZ])

    spread(0)
    densify()

    @pl.loop(0, TERMS - 1)
    def _(t):
        term(t)
        spread(t + 1)

    term(TERMS - 1)
    out[...] = score[...].T


def order_of(block_rows, block_cols, live, n_row, n_col):
    slots = block_rows.shape[0]
    every = jnp.arange(slots, dtype=jnp.int32)
    places = jnp.arange(n_row * n_col, dtype=jnp.int32)
    key = jnp.where(every < live, block_rows * n_col + block_cols, n_row * n_col)
    unique = key * slots + every
    rank = jnp.sum((unique[None, :] < unique[:, None]).astype(jnp.int32), axis=1)
    hit = rank[:, None] == every[None, :]
    order = jnp.sum(jnp.where(hit, every[:, None], 0), axis=0)
    keys = jnp.sum(jnp.where(hit, key[:, None], 0), axis=0)
    goes_on = jnp.concatenate([jnp.zeros((1,), jnp.int32), (keys[1:] == keys[:-1]).astype(jnp.int32)])
    upto = jnp.sum((key[:, None] <= places[None, :]).astype(jnp.int32), axis=0)
    there = jnp.sum((key[:, None] == places[None, :]).astype(jnp.int32), axis=0)
    ends = jnp.stack([jnp.maximum(upto - 1, 0), (there > 0).astype(jnp.int32)])
    return jnp.concatenate([jnp.stack([order, goes_on]), ends])


def shards(n_row, n_col, side, tiles, block_rows, block_cols, live, seeds, beta):
    tiles = tiles[0, 0]
    slots, blk, _ = tiles.shape
    width = seeds.shape[1]
    plane = side * side
    idx = order_of(block_rows[0, 0], block_cols[0, 0], live[0, 0], n_row, n_col)
    vmem = pl.BlockSpec(memory_space=pltpu.VMEM)
    return pl.pallas_call(
        functools.partial(kernel, side),
        out_shape=jax.ShapeDtypeStruct(seeds.shape, F32),
        in_specs=[
            pl.BlockSpec(memory_space=pltpu.SMEM),
            pl.BlockSpec(memory_space=pl.ANY),
            vmem,
            vmem,
        ],
        out_specs=vmem,
        scratch_shapes=[
            pltpu.VMEM((slots, blk, blk), BF16),
            pltpu.VMEM((slots, blk, blk), BF16),
            pltpu.VMEM((n_col, n_row * blk, blk), BF16),
            pltpu.VMEM((TERMS, n_col, width, blk), BF16),
            pltpu.VMEM((TERMS, n_row, width, blk), BF16),
            pltpu.VMEM((2, plane, width, blk), BF16),
            pltpu.VMEM((n_row, width, blk), BF16),
            pltpu.VMEM((TERMS, 2, plane, width, blk), BF16),
            pltpu.VMEM((TERMS, n_row, width, blk), BF16),
            pltpu.VMEM((width, blk), F32),
            pltpu.VMEM((TERMS, width, blk), F32),
            pltpu.VMEM((n_row // 2, 2 * blk, width), F32),
            pltpu.VMEM((width, blk), F32),
            pltpu.VMEM((width, blk), F32),
            pltpu.VMEM((width, blk), F32),
            pltpu.SemaphoreType.DMA((4,)),
            pltpu.SemaphoreType.DMA((TERMS, 8)),
            pltpu.SemaphoreType.DMA((TERMS, 8)),
        ],
        compiler_params=pltpu.CompilerParams(
            collective_id=0, has_side_effects=True, vmem_limit_bytes=56 << 20
        ),
        cost_estimate=pl.CostEstimate(
            flops=TERMS * 4 * n_row * n_col * blk * blk * width,
            bytes_accessed=2 * slots * blk * blk,
            transcendentals=0,
        ),
    )(idx, tiles, seeds, beta[None, :])


def solution(mesh):
    n_row, n_col = mesh.shape["row"], mesh.shape["col"]
    side = 1
    while 2 * side * side < n_col:
        side *= 2
    placed = (
        P("row", "col", None, None, None),
        P("row", "col", None),
        P("row", "col", None),
        P("row", "col"),
        P(("col", "row"), None),
        P(),
    )
    return jax.shard_map(
        functools.partial(shards, n_row, n_col, side),
        mesh=mesh,
        in_specs=placed,
        out_specs=P(("col", "row"), None),
        check_vma=False,
    )
```

time: 1690 us -> 99.1 us (0.06); the launches traced: 1660 us -> 98.9 us
  waiting for transfers between devices: 671 us -> 0 us
  blocking collectives: 467 us -> 0 us
  other arithmetic: 232 us -> 1.84 us
  matrix products: 180 us -> 0 us
  Pallas kernels: 0 us -> 93.4 us
  local copies, waits for them, and re-layouts: 94.4 us -> 3.01 us
    reduce_scatter x8 -> x0, waiting for transfers between devices: 671 us -> none  [the longest x4 563 us: shards(): lax.psum_scatter(backward, 'col', scatter_dimension=0, tiled=True)]
    all_gather x8 -> x0, blocking collectives: 467 us -> none  [the longest x4 269 us: shards(): across = lax.all_gather(current, 'col', axis=0, tiled=True)]
    dot_general x128 -> x0, matrix products: 180 us -> none  [the longest x64 96.3 us: add_group(): jnp.einsum('sij,sjk->sik', tile, incoming, preferred_element_type=jnp.flo...]
    scatter-add x128 -> x0, other arithmetic: 172 us -> none  [the longest x64 86.1 us: add_group(): forward = totals[0] + jax.ops.segment_sum(fwd, rows, row_blocks)]
    pallas_call x0 -> x1, Pallas kernels: none -> 93.4 us  [shards(): pl.pallas_call(functools.partial(kernel, side), out_shape=jax.ShapeDtypeS...]
    gather x128 -> x0, local copies, waits for them, and re-layouts: 76.6 us -> none  [the longest x64 38.3 us: add_group(): incoming = across.reshape(col_blocks, blk, width)[cols]]
    select_n x64 -> x0, other arithmetic: 49.7 us -> none  [add_group(): lowered = downward.reshape(row_blocks, blk, width)[rows]]
    reshape x136 -> x0, local copies, waits for them, and re-layouts: 17.4 us -> none  [the longest x64 8.62 us: add_group(): incoming = across.reshape(col_blocks, blk, width)[cols]]
  transfers between devices with their start and end apart: 8 -> 0, of which waited for: 8 -> 0; matrix products, arithmetic and copies ran while one was open for 0% -> 0% of each run, Pallas kernels for 0% -> 0%
where the time goes in v1:
time: 99.1 us; the launch traced here: 98.9 us
  Pallas kernels  93.4 us (94%)
  local copies, waits for them, and re-layouts  3.01 us (3%)
  other arithmetic  1.84 us (2%)
    pallas_call x1, Pallas kernels, shards(): pl.pallas_call(functools.partial(kernel, side), out_shape=jax.ShapeDtypeS...  93.4 us

profile of v1, /device:TPU:1, one launch (start us, length us, event | category | flops | bytes accessed | tf_op | source)
XLA Modules:
  0.0 98.9 jit_solution(3502530447972063126)
XLA Ops:
  0.7 0.7 multiply_add_fusion
  1.4 0.2 convert_reduce_fusion.2
  1.5 0.2 select_reduce_fusion.1
  1.7 0.1 slice_compare_fusion
  1.8 0.1 add_convert_fusion
  1.9 0.6 pad_add_fusion.idx
  2.5 1.5 %copy.9.seeds = f32[128,64]{1,0:T(8,128)} copy(f32[128,64]{0,1:T(8,128)} %param.10) | data formatting | bytes 65536 | tf_op args[4]
  4.0 93.4 %shard_map.64 = f32[128,64]{1,0:T(8,128)} custom-call(s32[4,256]{1,0:T(4,128)} %pad_add_fusion.idx, bf16[256,128,128]{2,1,0:T(8,128)(2,1)} %bitcast.14, f32[128,64]{1,0:T(8,128)} %copy.9.seeds, f32[1,64]{1,0:T(1,128)} %bitcast.15), custom_call_target="tpu_custom_call" | custom-call | flops 4294967296 | bytes 8388608 | tf_op jit(solution)/shard_map/pallas_call | solution.py:267
  97.3 1.5 %copy.10 = f32[128,64]{0,1:T(8,128)} copy(f32[128,64]{1,0:T(8,128)} %shard_map.64) | data formatting | bytes 65536 | tf_op jit(solution)/shard_map/pallas_call | solution.py:267
  (3 shorter events, 0.0 us)

commit v2 on v1

v2 whole, which is shorter than its diff:
```python
import functools

import jax
import jax.numpy as jnp
from jax import lax
from jax.experimental import pallas as pl
from jax.experimental.pallas import tpu as pltpu
from jax.sharding import PartitionSpec as P

TERMS = 4
MESH = pl.DeviceIdType.MESH
F32 = jnp.float32
BF16 = jnp.bfloat16
LAST = (((1,), (1,)), ((), ()))

XZ, XOWN, XOTHER, XSIB, XNEAR, XFAR, POTHER, POWN, PROW, PZ = range(10)


def far_first(side):
    steps = [(dy, dx) for dy in range(side) for dx in range(side)]
    return sorted(steps, key=lambda s: -min(s[0], side - s[0]) - min(s[1], side - s[1]))


def kernel(
    idx,
    tiles,
    seeds,
    beta,
    out,
    raw,
    run,
    dense,
    xs,
    ys,
    bacc,
    bstage,
    fstage,
    bland,
    fland,
    zstage,
    zland,
    facc,
    beta_t,
    score,
    tile_sem,
    send_sem,
    recv_sem,
):
    slots, blk, _ = raw.shape
    n_row = ys.shape[1]
    chips = n_row // 2
    plane = bstage.shape[1]
    side = round(plane**0.5)
    n_col = 2 * plane
    parts = tile_sem.shape[0]
    chunk = slots // parts
    steps = far_first(side)
    r = lax.axis_index("row")
    c = lax.axis_index("col")
    high, core = r // 2, r % 2
    sibling = (core + 1) % 2
    z = c // plane
    y = (c % plane) // side
    x = c % side
    other = (z + 1) % 2
    yx = y * side + x

    def stepped(i):
        dy, dx = steps[i]
        return ((y + dy) % side) * side + (x + dx) % side

    def chip(k):
        return (high + k) % chips

    def rows_of(k):
        return pl.ds(pl.multiple_of(chip(k) * 2 * blk, 2 * blk), 2 * blk)

    def tile_copy(i):
        part = pl.ds(i * chunk, chunk)
        return pltpu.make_async_copy(tiles.at[part], raw.at[part], tile_sem.at[i])

    for i in range(parts):
        tile_copy(i).start()

    def send(src, dst, t, kind, device):
        pltpu.make_async_remote_copy(
            src_ref=src,
            dst_ref=dst,
            send_sem=send_sem.at[t, kind],
            recv_sem=recv_sem.at[t, kind],
            device_id=device,
            device_id_type=MESH,
        ).start()

    def moved(t, kind):
        if kind in (XOWN, XOTHER, POTHER, POWN):
            return bland.at[t, 0, pl.ds(0, plane - 1)]
        if kind == PZ:
            return zland.at[t]
        count = {XZ: 1, XSIB: 1, XFAR: 2, XNEAR: n_row - 4, PROW: n_row - 1}[kind]
        return fland.at[t, pl.ds(0, count)]

    def arrived(t, kind):
        ref = moved(t, kind)
        pltpu.make_async_copy(ref, ref, recv_sem.at[t, kind]).wait()

    def left(t, kind):
        ref = moved(t, kind)
        pltpu.make_async_copy(ref, ref, send_sem.at[t, kind]).wait()

    barrier = pltpu.get_barrier_semaphore()

    def greet(device):
        pl.semaphore_signal(barrier, inc=1, device_id=device, device_id_type=MESH)

    for off in range(1, n_row):
        greet(((r + off) % n_row, c))
    for i in range(plane - 1):
        greet((r, z * plane + stepped(i)))
    greet((r, other * plane + yx))

    def add_slots():
        for i in range(parts):
            tile_copy(i).wait()

        def add(i, total):
            total = raw[idx[0, i]].astype(F32) + total * idx[1, i].astype(F32)
            run[i] = total.astype(BF16)
            return total

        lax.fori_loop(0, slots, add, jnp.zeros((blk, blk), F32), unroll=4)

    def place():
        @pl.loop(0, n_col)
        def _(cb):
            for rb in range(n_row):
                p = rb * n_col + cb
                dense[cb, rb * blk : (rb + 1) * blk, :] = run[idx[2, p]] * idx[3, p].astype(BF16)

    def spread(t):
        current = score[...].astype(BF16)
        ys[t, r] = current
        xs[t, c] = current
        piece = ys.at[t, r]
        for k in sorted(range(1, chips), key=lambda k: -min(k, chips - k)):
            kind = XFAR if 2 * k == chips else XNEAR
            for to in range(2):
                send(piece, piece, t, kind, (2 * chip(k) + to, c))
        send(piece, piece, t, XSIB, (2 * high + sibling, c))
        piece = xs.at[t, c]
        send(piece, piece, t, XZ, (r, other * plane + yx))
        for i in range(plane - 1):
            send(piece, piece, t, XOWN, (r, z * plane + stepped(i)))

    def pass_on(t):
        arrived(t, XZ)
        piece = xs.at[t, other * plane + yx]
        for i in range(plane - 1):
            send(piece, piece, t, XOTHER, (r, z * plane + stepped(i)))

    def pair(zz, g):
        return zz * plane + stepped(2 * g), zz * plane + stepped(2 * g + 1)

    def down(t, ks):
        return jnp.concatenate([ys[t, 2 * chip(k) + i] for k in ks for i in range(2)], axis=1)

    def block(zz, g, ks):
        one, two = pair(zz, g)
        both = [jnp.concatenate([dense[one, rows_of(k), :], dense[two, rows_of(k), :]], axis=1) for k in ks]
        return jnp.concatenate(both, axis=0)

    def transposed(t, ks, first):
        v = down(t, ks)
        for slot, zz in enumerate((other, z)):
            for g in range(plane // 2):
                part = jnp.dot(v, block(zz, g, ks), preferred_element_type=F32)
                bacc[slot, g] = part if first else bacc[slot, g] + part

    def transposed_last(t, ks):
        v = down(t, ks)
        for slot, zz, kind in ((0, other, POTHER), (1, z, POWN)):
            for g in range(plane // 2):
                part = jnp.dot(v, block(zz, g, ks), preferred_element_type=F32)
                part = (bacc[slot, g] + part).astype(BF16)
                bstage[slot, 2 * g] = part[:, :blk]
                bstage[slot, 2 * g + 1] = part[:, blk:]
                for i in (2 * g, 2 * g + 1):
                    if i < plane - 1:
                        send(bstage.at[slot, i], bland.at[t, slot, i], t, kind, (r, z * plane + stepped(i)))

    def forward(t, zz, last):
        for m, k in enumerate(sorted(range(chips), key=lambda k: -min(k, chips - k))):
            total = facc[m] if last else jnp.zeros(facc.shape[1:], F32)
            for p in range(plane // 2):
                at = zz * plane + 2 * p
                a = jnp.concatenate([dense[at, rows_of(k), :], dense[at + 1, rows_of(k), :]], axis=1)
                v = jnp.concatenate([xs[t, at], xs[t, at + 1]], axis=1)
                total = total + lax.dot_general(a, v, LAST, preferred_element_type=F32)
            if not last:
                facc[m] = total
                continue
            total = total.T.astype(BF16)
            fstage[2 * m] = total[:, :blk]
            fstage[2 * m + 1] = total[:, blk:]
            if k:
                for to in range(2):
                    send(fstage.at[2 * m + to], fland.at[t, 2 * m + core], t, PROW, (2 * chip(k) + to, c))
            else:
                send(fstage.at[2 * m + sibling], fland.at[t, 2 * m], t, PROW, (2 * high + sibling, c))

    def total_of(land, t, count, total):
        for i in range(count):
            total = total + land[t, i].astype(F32)
        return total

    beta_t[...] = jnp.broadcast_to(beta[...], (blk, beta.shape[1])).T
    score[...] = seeds[...]
    add_slots()
    pl.semaphore_wait(barrier, (n_row - 1) + (plane - 1) + 1)
    spread(0)
    place()

    @pl.loop(0, TERMS)
    def _(t):
        arrived(t, XSIB)
        transposed(t, (0,), True)
        pass_on(t)
        near = tuple(k for k in range(1, chips) if 2 * k != chips)
        if near:
            arrived(t, XNEAR)
            transposed(t, near, False)
        arrived(t, XFAR)
        transposed_last(t, (chips // 2,))
        arrived(t, XOWN)
        forward(t, z, False)
        arrived(t, XOTHER)
        forward(t, other, True)
        arrived(t, POTHER)
        zstage[...] = total_of(bland.at[:, 0], t, plane - 1, bstage[0, plane - 1].astype(F32))
        send(zstage, zland.at[t], t, PZ, (r, other * plane + yx))
        arrived(t, POWN)
        total = total_of(bland.at[:, 1], t, plane - 1, bstage[1, plane - 1].astype(F32))
        arrived(t, PROW)
        total = total_of(fland, t, n_row - 1, total + fstage[n_row - 2 + core].astype(F32))
        arrived(t, PZ)
        total = total + zland[t]
        score[...] = beta_t[...] * total + seeds[...]

        for kind in range(10):
            if kind != XNEAR or near:
                left(t, kind)

        @pl.when(t < TERMS - 1)
        def _():
            spread(t + 1)

    out[...] = score[...]


def order_of(block_rows, block_cols, live, n_row, n_col):
    slots = block_rows.shape[0]
    every = jnp.arange(slots, dtype=jnp.int32)
    places = jnp.arange(n_row * n_col, dtype=jnp.int32)
    key = jnp.where(every < live, block_rows * n_col + block_cols, n_row * n_col)
    unique = key * slots + every
    rank = jnp.sum((unique[None, :] < unique[:, None]).astype(jnp.int32), axis=1)
    hit = rank[:, None] == every[None, :]
    order = jnp.sum(jnp.where(hit, every[:, None], 0), axis=0)
    keys = jnp.sum(jnp.where(hit, key[:, None], 0), axis=0)
    goes_on = jnp.concatenate([jnp.zeros((1,), jnp.int32), (keys[1:] == keys[:-1]).astype(jnp.int32)])
    upto = jnp.sum((key[:, None] <= places[None, :]).astype(jnp.int32), axis=0)
    there = jnp.sum((key[:, None] == places[None, :]).astype(jnp.int32), axis=0)
    ends = jnp.stack([jnp.maximum(upto - 1, 0), (there > 0).astype(jnp.int32)])
    return jnp.concatenate([jnp.stack([order, goes_on]), ends])


def shards(n_row, n_col, tiles, block_rows, block_cols, live, seeds, beta):
    tiles = tiles[0, 0]
    slots, blk, _ = tiles.shape
    width = seeds.shape[1]
    plane = n_col // 2
    idx = order_of(block_rows[0, 0], block_cols[0, 0], live[0, 0], n_row, n_col)
    vmem = pl.BlockSpec(memory_space=pltpu.VMEM)
    scores = pl.pallas_call(
        kernel,
        out_shape=jax.ShapeDtypeStruct((width, blk), F32),
        in_specs=[
            pl.BlockSpec(memory_space=pltpu.SMEM),
            pl.BlockSpec(memory_space=pl.ANY),
            vmem,
            vmem,
        ],
        out_specs=vmem,
        scratch_shapes=[
            pltpu.VMEM((slots, blk, blk), BF16),
            pltpu.VMEM((slots, blk, blk), BF16),
            pltpu.VMEM((n_col, n_row * blk, blk), BF16),
            pltpu.VMEM((TERMS, n_col, width, blk), BF16),
            pltpu.VMEM((TERMS, n_row, width, blk), BF16),
            pltpu.VMEM((2, plane // 2, width, 2 * blk), F32),
            pltpu.VMEM((2, plane, width, blk), BF16),
            pltpu.VMEM((n_row, width, blk), BF16),
            pltpu.VMEM((TERMS, 2, plane - 1, width, blk), BF16),
            pltpu.VMEM((TERMS, n_row - 1, width, blk), BF16),
            pltpu.VMEM((width, blk), F32),
            pltpu.VMEM((TERMS, width, blk), F32),
            pltpu.VMEM((n_row // 2, 2 * blk, width), F32),
            pltpu.VMEM((width, blk), F32),
            pltpu.VMEM((width, blk), F32),
            pltpu.SemaphoreType.DMA((4,)),
            pltpu.SemaphoreType.DMA((TERMS, 10)),
            pltpu.SemaphoreType.DMA((TERMS, 10)),
        ],
        compiler_params=pltpu.CompilerParams(
            collective_id=0, has_side_effects=True, vmem_limit_bytes=56 << 20
        ),
        cost_estimate=pl.CostEstimate(
            flops=TERMS * 4 * n_row * n_col * blk * blk * width,
            bytes_accessed=2 * slots * blk * blk,
            transcendentals=0,
        ),
    )(idx, tiles, seeds.T, beta[None, :])
    return scores.T


def solution(mesh):
    n_row, n_col = mesh.shape["row"], mesh.shape["col"]
    placed = (
        P("row", "col", None, None, None),
        P("row", "col", None),
        P("row", "col", None),
        P("row", "col"),
        P(("col", "row"), None),
        P(),
    )
    return jax.shard_map(
        functools.partial(shards, n_row, n_col),
        mesh=mesh,
        in_specs=placed,
        out_specs=P(("col", "row"), None),
        check_vma=False,
    )
```

time: 99.1 us -> 89.4 us (0.902)
  Pallas kernels: 93.4 us -> 85.2 us
  local copies, waits for them, and re-layouts: 3.01 us -> 1.38 us
    pallas_call x1, Pallas kernels: 93.4 us -> 85.2 us  [shards(): pl.pallas_call(kernel, out_shape=jax.ShapeDtypeStruct((width, blk), F32),...]
    pallas_call x1 -> x0, local copies, waits for them, and re-layouts: 1.54 us -> none  [shards(): pl.pallas_call(functools.partial(kernel, side), out_shape=jax.ShapeDtypeS...]
where the time goes in v2:
time: 89.4 us; the launch traced here: 89.1 us
  Pallas kernels  85.2 us (95%)
  other arithmetic  1.84 us (2%)
  local copies, waits for them, and re-layouts  1.38 us (2%)
    pallas_call x1, Pallas kernels, shards(): pl.pallas_call(kernel, out_shape=jax.ShapeDtypeStruct((width, blk), F32),...  85.2 us

profile of v2, /device:TPU:1, one launch (start us, length us, event | category | flops | bytes accessed | tf_op | source)
XLA Modules:
  0.0 89.1 jit_solution(839289301229943507)
XLA Ops:
  0.7 0.7 multiply_add_fusion
  1.4 0.2 convert_reduce_fusion.2
  1.5 0.2 select_reduce_fusion.1
  1.7 0.1 slice_compare_fusion
  1.8 0.1 add_convert_fusion
  1.9 0.6 pad_add_fusion.idx
  2.5 85.2 %shard_map.64 = f32[64,128]{1,0:T(8,128)} custom-call(s32[4,256]{1,0:T(4,128)} %pad_add_fusion.idx, bf16[256,128,128]{2,1,0:T(8,128)(2,1)} %bitcast.17, f32[64,128]{1,0:T(8,128)} %bitcast.18, f32[1,64]{1,0:T(1,128)} %bitcast.19), custom_call_target="tpu_custom_call" | custom-call | flops 4294967296 | bytes 8388608 | tf_op jit(solution)/shard_map/pallas_call | solution.py:284
  87.7 1.4 %copy.9 = f32[128,64]{0,1:T(8,128)} copy(f32[128,64]{0,1:T(8,128)} %bitcast.11) | data formatting | bytes 65536
  (3 shorter events, 0.0 us)

commit v3 on v2

--- a/solution.py
+++ b/solution.py
@@ -22,7 +22,9 @@
 
 
 def kernel(
-    idx,
+    live,
+    block_rows,
+    block_cols,
     tiles,
     seeds,
     beta,
@@ -42,6 +44,9 @@
     facc,
     beta_t,
     score,
+    table,
+    idx,
+    table_sem,
     tile_sem,
     send_sem,
     recv_sem,
@@ -119,6 +124,30 @@
         greet((r, z * plane + stepped(i)))
     greet((r, other * plane + yx))
 
+    def order_slots():
+        n = slots
+        along = lax.broadcasted_iota(jnp.int32, (1, n), 1)
+        key = jnp.where(along < live[...], block_rows[...] * n_col + block_cols[...], n_row * n_col)
+        keys = jnp.broadcast_to(key, (n, n))
+        keys_down = keys.T
+        across = lax.broadcasted_iota(jnp.int32, (n, n), 1)
+        down = lax.broadcasted_iota(jnp.int32, (n, n), 0)
+        ahead = (keys_down < keys) | ((keys_down == keys) & (down < across))
+        rank = jnp.sum(ahead.astype(jnp.int32), axis=0, keepdims=True)
+        hit = jnp.broadcast_to(rank, (n, n)).T == across
+        order = jnp.sum(jnp.where(hit, down, 0), axis=0, keepdims=True)
+        placed = jnp.sum(jnp.where(hit, keys_down, 0), axis=0, keepdims=True)
+        goes_on = (placed == pltpu.roll(placed, 1, axis=1)) & (along > 0)
+        upto = jnp.sum((keys_down <= across).astype(jnp.int32), axis=0, keepdims=True)
+        there = jnp.sum((keys_down == across).astype(jnp.int32), axis=0, keepdims=True)
+        table[0:1, :] = order
+        table[1:2, :] = goes_on.astype(jnp.int32)
+        table[2:3, :] = jnp.maximum(upto - 1, 0)
+        table[3:4, :] = (there > 0).astype(jnp.int32)
+        copy = pltpu.make_async_copy(table, idx, table_sem)
+        copy.start()
+        copy.wait()
+
     def add_slots():
         for i in range(parts):
             tile_copy(i).wait()
@@ -141,6 +170,8 @@
         current = score[...].astype(BF16)
         ys[t, r] = current
         xs[t, c] = current
+        piece = xs.at[t, c]
+        send(piece, piece, t, XZ, (r, other * plane + yx))
         piece = ys.at[t, r]
         for k in sorted(range(1, chips), key=lambda k: -min(k, chips - k)):
             kind = XFAR if 2 * k == chips else XNEAR
@@ -148,7 +179,6 @@
                 send(piece, piece, t, kind, (2 * chip(k) + to, c))
         send(piece, piece, t, XSIB, (2 * high + sibling, c))
         piece = xs.at[t, c]
-        send(piece, piece, t, XZ, (r, other * plane + yx))
         for i in range(plane - 1):
             send(piece, piece, t, XOWN, (r, z * plane + stepped(i)))
 
@@ -169,24 +199,23 @@
         both = [jnp.concatenate([dense[one, rows_of(k), :], dense[two, rows_of(k), :]], axis=1) for k in ks]
         return jnp.concatenate(both, axis=0)
 
-    def transposed(t, ks, first):
+    def transposed(t, planes, ks, first):
         v = down(t, ks)
-        for slot, zz in enumerate((other, z)):
+        for slot, zz in planes:
             for g in range(plane // 2):
                 part = jnp.dot(v, block(zz, g, ks), preferred_element_type=F32)
                 bacc[slot, g] = part if first else bacc[slot, g] + part
 
-    def transposed_last(t, ks):
+    def transposed_last(t, slot, zz, ks, kind):
         v = down(t, ks)
-        for slot, zz, kind in ((0, other, POTHER), (1, z, POWN)):
-            for g in range(plane // 2):
-                part = jnp.dot(v, block(zz, g, ks), preferred_element_type=F32)
-                part = (bacc[slot, g] + part).astype(BF16)
-                bstage[slot, 2 * g] = part[:, :blk]
-                bstage[slot, 2 * g + 1] = part[:, blk:]
-                for i in (2 * g, 2 * g + 1):
-                    if i < plane - 1:
-                        send(bstage.at[slot, i], bland.at[t, slot, i], t, kind, (r, z * plane + stepped(i)))
+        for g in range(plane // 2):
+            part = jnp.dot(v, block(zz, g, ks), preferred_element_type=F32)
+            part = (bacc[slot, g] + part).astype(BF16)
+            bstage[slot, 2 * g] = part[:, :blk]
+            bstage[slot, 2 * g + 1] = part[:, blk:]
+            for i in (2 * g, 2 * g + 1):
+                if i < plane - 1:
+                    send(bstage.at[slot, i], bland.at[t, slot, i], t, kind, (r, z * plane + stepped(i)))
 
     def forward(t, zz, last):
         for m, k in enumerate(sorted(range(chips), key=lambda k: -min(k, chips - k))):
@@ -213,65 +242,56 @@
             total = total + land[t, i].astype(F32)
         return total
 
+    def begin(t):
+        arrived(t, XSIB)
+        transposed(t, ((0, other), (1, z)), (0,), True)
+
     beta_t[...] = jnp.broadcast_to(beta[...], (blk, beta.shape[1])).T
     score[...] = seeds[...]
-    add_slots()
     pl.semaphore_wait(barrier, (n_row - 1) + (plane - 1) + 1)
     spread(0)
+    order_slots()
+    add_slots()
+    pass_on(0)
     place()
+    begin(0)
 
     @pl.loop(0, TERMS)
     def _(t):
-        arrived(t, XSIB)
-        transposed(t, (0,), True)
-        pass_on(t)
         near = tuple(k for k in range(1, chips) if 2 * k != chips)
         if near:
             arrived(t, XNEAR)
-            transposed(t, near, False)
+            transposed(t, ((0, other), (1, z)), near, False)
         arrived(t, XFAR)
-        transposed_last(t, (chips // 2,))
+        transposed_last(t, 0, other, (chips // 2,), POTHER)
+        transposed_last(t, 1, z, (chips // 2,), POWN)
         arrived(t, XOWN)
         forward(t, z, False)
         arrived(t, XOTHER)
         forward(t, other, True)
         arrived(t, POTHER)
-        zstage[...] = total_of(bland.at[:, 0], t, plane - 1, bstage[0, plane - 1].astype(F32))
+        crossing = total_of(bland.at[:, 0], t, plane - 1, bstage[0, plane - 1].astype(F32))
+        zstage[...] = crossing.astype(BF16)
         send(zstage, zland.at[t], t, PZ, (r, other * plane + yx))
         arrived(t, POWN)
         total = total_of(bland.at[:, 1], t, plane - 1, bstage[1, plane - 1].astype(F32))
         arrived(t, PROW)
         total = total_of(fland, t, n_row - 1, total + fstage[n_row - 2 + core].astype(F32))
         arrived(t, PZ)
-        total = total + zland[t]
+        total = total + zland[t].astype(F32)
         score[...] = beta_t[...] * total + seeds[...]
+
+        @pl.when(t < TERMS - 1)
+        def _():
+            spread(t + 1)
+            begin(t + 1)
+            pass_on(t + 1)
 
         for kind in range(10):
             if kind != XNEAR or near:
                 left(t, kind)
 
-        @pl.when(t < TERMS - 1)
-        def _():
-            spread(t + 1)
-
     out[...] = score[...]
-
-
-def order_of(block_rows, block_cols, live, n_row, n_col):
-    slots = block_rows.shape[0]
-    every = jnp.arange(slots, dtype=jnp.int32)
-    places = jnp.arange(n_row * n_col, dtype=jnp.int32)
-    key = jnp.where(every < live, block_rows * n_col + block_cols, n_row * n_col)
-    unique = key * slots + every
-    rank = jnp.sum((unique[None, :] < unique[:, None]).astype(jnp.int32), axis=1)
-    hit = rank[:, None] == every[None, :]
-    order = jnp.sum(jnp.where(hit, every[:, None], 0), axis=0)
-    keys = jnp.sum(jnp.where(hit, key[:, None], 0), axis=0)
-    goes_on = jnp.concatenate([jnp.zeros((1,), jnp.int32), (keys[1:] == keys[:-1]).astype(jnp.int32)])
-    upto = jnp.sum((key[:, None] <= places[None, :]).astype(jnp.int32), axis=0)
-    there = jnp.sum((key[:, None] == places[None, :]).astype(jnp.int32), axis=0)
-    ends = jnp.stack([jnp.maximum(upto - 1, 0), (there > 0).astype(jnp.int32)])
-    return jnp.concatenate([jnp.stack([order, goes_on]), ends])
 
 
 def shards(n_row, n_col, tiles, block_rows, block_cols, live, seeds, beta):
@@ -279,13 +299,15 @@
     slots, blk, _ = tiles.shape
     width = seeds.shape[1]
     plane = n_col // 2
-    idx = order_of(block_rows[0, 0], block_cols[0, 0], live[0, 0], n_row, n_col)
+    assert slots == n_row * n_col
     vmem = pl.BlockSpec(memory_space=pltpu.VMEM)
     scores = pl.pallas_call(
         kernel,
         out_shape=jax.ShapeDtypeStruct((width, blk), F32),
         in_specs=[
-            pl.BlockSpec(memory_space=pltpu.SMEM),
+            vmem,
+            vmem,
+            vmem,
             pl.BlockSpec(memory_space=pl.ANY),
             vmem,
             vmem,
@@ -302,11 +324,14 @@
             pltpu.VMEM((n_row, width, blk), BF16),
             pltpu.VMEM((TERMS, 2, plane - 1, width, blk), BF16),
             pltpu.VMEM((TERMS, n_row - 1, width, blk), BF16),
-            pltpu.VMEM((width, blk), F32),
-            pltpu.VMEM((TERMS, width, blk), F32),
+            pltpu.VMEM((width, blk), BF16),
+            pltpu.VMEM((TERMS, width, blk), BF16),
             pltpu.VMEM((n_row // 2, 2 * blk, width), F32),
             pltpu.VMEM((width, blk), F32),
             pltpu.VMEM((width, blk), F32),
+            pltpu.VMEM((8, slots), jnp.int32),
+            pltpu.SMEM((8, slots), jnp.int32),
+            pltpu.SemaphoreType.DMA,
             pltpu.SemaphoreType.DMA((4,)),
             pltpu.SemaphoreType.DMA((TERMS, 10)),
             pltpu.SemaphoreType.DMA((TERMS, 10)),
@@ -319,7 +344,7 @@
             bytes_accessed=2 * slots * blk * blk,
             transcendentals=0,
         ),
-    )(idx, tiles, seeds.T, beta[None, :])
+    )(live, block_rows[0], block_cols[0], tiles, seeds.T, beta[None, :])
     return scores.T
 
 

time: 89.4 us -> 84.2 us (0.942)
  Pallas kernels: 85.2 us -> 81.9 us
  other arithmetic: 1.84 us -> 0 us
    pallas_call x1, Pallas kernels: 85.2 us -> 81.9 us  [shards(): pl.pallas_call(kernel, out_shape=jax.ShapeDtypeStruct((width, blk), F32),...]
where the time goes in v3:
time: 84.2 us; the launch traced here: 83.9 us
  Pallas kernels  81.9 us (97%)
  local copies, waits for them, and re-layouts  1.38 us (2%)
    pallas_call x1, Pallas kernels, shards(): pl.pallas_call(kernel, out_shape=jax.ShapeDtypeStruct((width, blk), F32),...  81.9 us

profile of v3, /device:TPU:1, one launch (start us, length us, event | category | flops | bytes accessed | tf_op | source)
XLA Modules:
  0.0 83.9 jit_solution(17260250654636831000)
XLA Ops:
  0.7 81.9 %shard_map.64 = f32[64,128]{1,0:T(8,128)} custom-call(s32[1,1]{1,0:T(1,128)S(6)} %copy.8.live, s32[1,256]{1,0:T(1,128)} %bitcast.9, s32[1,256]{1,0:T(1,128)} %bitcast.10, bf16[256,128,128]{2,1,0:T(8,128)(2,1)} %bitcast.7, f32[64,128]{1,0:T(8,128)} %bitcast.8, f32[1,64]{1,0:T(1,128)} %bitcast.11), custom_call_target="tpu_custom_call" | custom-call | flops 4294967296 | bytes 8388608 | tf_op jit(solution)/shard_map/pallas_call | solution.py:304
  82.6 1.4 %copy.9 = f32[128,64]{0,1:T(8,128)} copy(f32[128,64]{0,1:T(8,128)} %bitcast.6) | data formatting | bytes 65536

commit v4 on v3

--- a/solution.py
+++ b/solution.py
@@ -18,7 +18,7 @@
 
 def far_first(side):
     steps = [(dy, dx) for dy in range(side) for dx in range(side)]
-    return sorted(steps, key=lambda s: -min(s[0], side - s[0]) - min(s[1], side - s[1]))
+    return sorted(steps, key=lambda s: (-min(s[0], side - s[0]) - min(s[1], side - s[1]), 0 in s))
 
 
 def kernel(
@@ -214,8 +214,12 @@
             bstage[slot, 2 * g] = part[:, :blk]
             bstage[slot, 2 * g + 1] = part[:, blk:]
             for i in (2 * g, 2 * g + 1):
-                if i < plane - 1:
+                if slot == 0 and i < plane - 1:
                     send(bstage.at[slot, i], bland.at[t, slot, i], t, kind, (r, z * plane + stepped(i)))
+
+    def ship_own(t, which):
+        for i in which:
+            send(bstage.at[1, i], bland.at[t, 1, i], t, POWN, (r, z * plane + stepped(i)))
 
     def forward(t, zz, last):
         for m, k in enumerate(sorted(range(chips), key=lambda k: -min(k, chips - k))):
@@ -234,6 +238,8 @@
             if k:
                 for to in range(2):
                     send(fstage.at[2 * m + to], fland.at[t, 2 * m + core], t, PROW, (2 * chip(k) + to, c))
+                if m == 0:
+                    ship_own(t, range(plane - 1))
             else:
                 send(fstage.at[2 * m + sibling], fland.at[t, 2 * m], t, PROW, (2 * high + sibling, c))
 
@@ -264,9 +270,9 @@
             transposed(t, ((0, other), (1, z)), near, False)
         arrived(t, XFAR)
         transposed_last(t, 0, other, (chips // 2,), POTHER)
-        transposed_last(t, 1, z, (chips // 2,), POWN)
         arrived(t, XOWN)
         forward(t, z, False)
+        transposed_last(t, 1, z, (chips // 2,), POWN)
         arrived(t, XOTHER)
         forward(t, other, True)
         arrived(t, POTHER)

time: 84.2 us -> 80.3 us (0.954)
  Pallas kernels: 81.9 us -> 78 us
    pallas_call x1, Pallas kernels: 81.9 us -> 78 us  [shards(): pl.pallas_call(kernel, out_shape=jax.ShapeDtypeStruct((width, blk), F32),...]
where the time goes in v4:
time: 80.3 us; the launch traced here: 80.1 us
  Pallas kernels  78 us (97%)
  local copies, waits for them, and re-layouts  1.38 us (2%)
    pallas_call x1, Pallas kernels, shards(): pl.pallas_call(kernel, out_shape=jax.ShapeDtypeStruct((width, blk), F32),...  78 us

profile of v4, /device:TPU:1, one launch (start us, length us, event | category | flops | bytes accessed | tf_op | source)
XLA Modules:
  0.0 80.1 jit_solution(1174116843332217234)
XLA Ops:
  0.7 78.0 %shard_map.64 = f32[64,128]{1,0:T(8,128)} custom-call(s32[1,1]{1,0:T(1,128)S(6)} %copy.8.live, s32[1,256]{1,0:T(1,128)} %bitcast.9, s32[1,256]{1,0:T(1,128)} %bitcast.10, bf16[256,128,128]{2,1,0:T(8,128)(2,1)} %bitcast.7, f32[64,128]{1,0:T(8,128)} %bitcast.8, f32[1,64]{1,0:T(1,128)} %bitcast.11), custom_call_target="tpu_custom_call" | custom-call | flops 4294967296 | bytes 8388608 | tf_op jit(solution)/shard_map/pallas_call | solution.py:310
  78.7 1.4 %copy.9 = f32[128,64]{0,1:T(8,128)} copy(f32[128,64]{0,1:T(8,128)} %bitcast.6) | data formatting | bytes 65536

commit v5 on v4

--- a/solution.py
+++ b/solution.py
@@ -173,11 +173,11 @@
         piece = xs.at[t, c]
         send(piece, piece, t, XZ, (r, other * plane + yx))
         piece = ys.at[t, r]
+        send(piece, piece, t, XSIB, (2 * high + sibling, c))
         for k in sorted(range(1, chips), key=lambda k: -min(k, chips - k)):
             kind = XFAR if 2 * k == chips else XNEAR
             for to in range(2):
                 send(piece, piece, t, kind, (2 * chip(k) + to, c))
-        send(piece, piece, t, XSIB, (2 * high + sibling, c))
         piece = xs.at[t, c]
         for i in range(plane - 1):
             send(piece, piece, t, XOWN, (r, z * plane + stepped(i)))
@@ -277,14 +277,14 @@
         forward(t, other, True)
         arrived(t, POTHER)
         crossing = total_of(bland.at[:, 0], t, plane - 1, bstage[0, plane - 1].astype(F32))
-        zstage[...] = crossing.astype(BF16)
+        zstage[...] = crossing
         send(zstage, zland.at[t], t, PZ, (r, other * plane + yx))
         arrived(t, POWN)
         total = total_of(bland.at[:, 1], t, plane - 1, bstage[1, plane - 1].astype(F32))
         arrived(t, PROW)
         total = total_of(fland, t, n_row - 1, total + fstage[n_row - 2 + core].astype(F32))
         arrived(t, PZ)
-        total = total + zland[t].astype(F32)
+        total = total + zland[t]
         score[...] = beta_t[...] * total + seeds[...]
 
         @pl.when(t < TERMS - 1)
@@ -330,8 +330,8 @@
             pltpu.VMEM((n_row, width, blk), BF16),
             pltpu.VMEM((TERMS, 2, plane - 1, width, blk), BF16),
             pltpu.VMEM((TERMS, n_row - 1, width, blk), BF16),
-            pltpu.VMEM((width, blk), BF16),
-            pltpu.VMEM((TERMS, width, blk), BF16),
+            pltpu.VMEM((width, blk), F32),
+            pltpu.VMEM((TERMS, width, blk), F32),
             pltpu.VMEM((n_row // 2, 2 * blk, width), F32),
             pltpu.VMEM((width, blk), F32),
             pltpu.VMEM((width, blk), F32),

time: 80.3 us -> 80.5 us (level)
  no operation moved by 1% of the time
where the time goes in v5:
time: 80.5 us; the launch traced here: 80.3 us
  Pallas kernels  78.3 us (97%)
  local copies, waits for them, and re-layouts  1.38 us (2%)
    pallas_call x1, Pallas kernels, shards(): pl.pallas_call(kernel, out_shape=jax.ShapeDtypeStruct((width, blk), F32),...  78.3 us

profile of v5, /device:TPU:1, one launch (start us, length us, event | category | flops | bytes accessed | tf_op | source)
XLA Modules:
  0.0 80.3 jit_solution(7283319361511722041)
XLA Ops:
  0.7 78.3 %shard_map.64 = f32[64,128]{1,0:T(8,128)} custom-call(s32[1,1]{1,0:T(1,128)S(6)} %copy.8.live, s32[1,256]{1,0:T(1,128)} %bitcast.9, s32[1,256]{1,0:T(1,128)} %bitcast.10, bf16[256,128,128]{2,1,0:T(8,128)(2,1)} %bitcast.7, f32[64,128]{1,0:T(8,128)} %bitcast.8, f32[1,64]{1,0:T(1,128)} %bitcast.11), custom_call_target="tpu_custom_call" | custom-call | flops 4294967296 | bytes 8388608 | tf_op jit(solution)/shard_map/pallas_call | solution.py:310
  78.9 1.4 %copy.9 = f32[128,64]{0,1:T(8,128)} copy(f32[128,64]{0,1:T(8,128)} %bitcast.6) | data formatting | bytes 65536
